TPU v7x, 256 devices: a whole 4x4x8 slice. The times are simulated.
256 devices in a mesh: ctx: 32 (over z, x), kvh: 8 (over y, core).
Axes of the slice: x: 4, y: 4, z: 8, core: 2. Of those that a mesh axis runs over, the one named last changes fastest.
Arguments:
- queries: float32 [256, 8192], P('ctx', 'kvh'), may hold values from -10 to 10
- cache_keys: float32 [131072, 1024], P('ctx', 'kvh'), may hold values from -12 to 12
- cache_values: float32 [131072, 1024], P('ctx', 'kvh'), may hold values from -6 to 6
- new_keys: float32 [256, 1024], P('ctx', 'kvh'), may hold values from -16 to 16
- new_values: float32 [256, 1024], P('ctx', 'kvh'), may hold values from -6 to 6
- block_lengths: int32 [32], P('ctx'), may hold values from 1 to 4096, 98304 in all
Outputs:
- attended: float32 [256, 8192], P(('ctx', 'kvh'))
All inputs are finite; a program needn't handle non-finite values. No bound on the sum of `block_lengths` on one device may be relied on, other than what follows from the above.
Results may differ from a plain program's by a relative error of at most 0.0003.
Values sent between devices are 32-bit elements; how exact they have to be, the bound alone decides.
A program may use at most 128 MiB of HBM per device.

v0:
```python
import jax
import jax.numpy as jnp
from jax import lax
from jax.sharding import PartitionSpec as P

HQ = 64
KVH = 8
HD = 128


def fold_block(carry, scores, values):
    peak, total, accum = carry
    new_peak = jnp.maximum(peak, jnp.max(scores, axis=-1))
    weights = jnp.exp(scores - new_peak[..., None])
    factor = jnp.exp(peak - new_peak)
    total = total * factor + jnp.sum(weights, axis=-1)
    accum = accum * factor[..., None] + jnp.einsum(
        "kgtj,jkd->kgtd", weights, values, precision=lax.Precision.HIGHEST
    )
    return (new_peak, total, accum)


def per_device(queries, cache_keys, cache_values, new_keys, new_values, block_lengths):
    group = HQ // KVH
    scale = 1.0 / HD**0.5
    slots = cache_keys.shape[0]
    kv_local = cache_keys.shape[1] // HD
    own_rows = queries.shape[0]
    width = min(512, slots)
    whole_q = lax.all_gather(queries, "ctx", axis=0, tiled=True)
    total_rows = whole_q.shape[0]
    query_heads = whole_q.reshape(total_rows, kv_local, group, HD)
    keys_blocks = cache_keys.reshape(slots // width, width, kv_local, HD)
    value_blocks = cache_values.reshape(slots // width, width, kv_local, HD)
    filled = block_lengths[0]
    count = (filled + width - 1) // width

    def key_step(index, carry):
        block_k = lax.dynamic_index_in_dim(keys_blocks, index, 0, keepdims=False)
        block_v = lax.dynamic_index_in_dim(value_blocks, index, 0, keepdims=False)
        scores = (
            jnp.einsum("tkgd,jkd->kgtj", query_heads, block_k, precision=lax.Precision.HIGHEST)
            * scale
        )
        places = index * width + jnp.arange(width, dtype=jnp.int32)
        scores = jnp.where((places < filled)[None, None, None, :], scores, -1e30)
        return fold_block(carry, scores, block_v)

    init = (
        jnp.full((kv_local, group, total_rows), -1e30, jnp.float32),
        jnp.zeros((kv_local, group, total_rows), jnp.float32),
        jnp.zeros((kv_local, group, total_rows, HD), jnp.float32),
    )
    peak, total, accum = lax.fori_loop(0, count, key_step, init)
    start = lax.axis_index("ctx") * own_rows
    peaks, totals, accums = (
        lax.all_to_all(peak[None], "ctx", split_axis=3, concat_axis=0, tiled=True),
        lax.all_to_all(total[None], "ctx", split_axis=3, concat_axis=0, tiled=True),
        lax.all_to_all(accum[None], "ctx", split_axis=3, concat_axis=0, tiled=True),
    )
    peak = jnp.max(peaks, axis=0)
    factor = jnp.exp(peaks - peak[None])
    total = jnp.sum(totals * factor, axis=0)
    accum = jnp.sum(accums * factor[..., None], axis=0)
    block_k, block_v = (
        lax.all_gather(new_keys, "ctx", axis=0, tiled=True),
        lax.all_gather(new_values, "ctx", axis=0, tiled=True),
    )
    block_k = block_k.reshape(total_rows, kv_local, HD)
    block_v = block_v.reshape(total_rows, kv_local, HD)
    local_q = queries.reshape(own_rows, kv_local, group, HD)
    scores = jnp.einsum("tkgd,jkd->kgtj", local_q, block_k, precision=lax.Precision.HIGHEST) * scale
    row_index = start + jnp.arange(own_rows, dtype=jnp.int32)
    key_index = jnp.arange(total_rows, dtype=jnp.int32)
    visible = key_index[None, :] <= row_index[:, None]
    scores = jnp.where(visible[None, None], scores, -1e30)
    peak, total, accum = fold_block((peak, total, accum), scores, block_v)
    result = (
        (accum / total[..., None]).transpose(2, 0, 1, 3).reshape(own_rows, kv_local * group * HD)
    )
    return lax.all_to_all(result, "kvh", split_axis=0, concat_axis=1, tiled=True)


def solution(mesh):
    in_specs = (
        P("ctx", "kvh"),
        P("ctx", "kvh"),
        P("ctx", "kvh"),
        P("ctx", "kvh"),
        P("ctx", "kvh"),
        P("ctx"),
    )
    out_specs = P(("ctx", "kvh"), None)
    return jax.shard_map(
        per_device, mesh=mesh, in_specs=in_specs, out_specs=out_specs, check_vma=False
    )
```

profile of v0, /device:TPU:1, one launch (start us, length us, event | category | flops | bytes accessed | tf_op | source)
XLA Modules:
  0.0 360.5 jit_solution(18178158634767835974)
XLA Ops:
  7.9 77.6 %all-gather.2.cloned.1.call-done = f32[256,1024]{1,0:T(8,128)} async-done(((f32[8,1024]{1,0:T(8,128)}), f32[256,1024]{1,0:T(8,128)}) %all-gather.2.cloned.1.call-update) | async-done | bytes 1048592 | tf_op jit(solution)/shard_map/all_gather | solution.py:30
  85.5 1.6 copy.49
  87.5 103.9 %while.14 = (s32[]{:T(128)}, f32[1,8,256]{2,1,0:T(8,128)S(1)}, f32[1,8,256]{2,1,0:T(8,128)S(1)}, f32[1,8,256,128]{3,2,1,0:T(8,128)S(1)}, s32[]{:T(128)}, /*index...) while((s32[]{:T(128)}, f32[1,8,256]{2,1,0:T(8,128)S(1)}, ...), condition=%wide.region_3.4_spmd, body=%wide.region_0.3_spmd.sunk | while | flops 3232242688 | bytes 16386235 | solution.py:54
  88.2 4.8 %bitcast_reduce_fusion.3 = (f32[8,256]{1,0:T(8,128)S(1)}, f32[512,256,8]{1,0,2:T(8,128)S(1)}) fusion(pred[512]{0:T(512)(128)(4,1)S(1)} %add_compare_fusion.2, f32[256,1,8,128]{3,0,2,1:T(8,128)S(1)} %get-tuple-element.219, f32[8,512,1,128]{3,1,2,0:T(8,128)} %get-tuple-element.218, s32[]{:T(128)S(6)} %select_n.45), kind=kOutput, calls=%fused_computation.3.clone.1 | convolution fusion | flops 1613756416 | bytes 5513732 | tf_op jit(solution)/shard_map/while/body/tkgd,jkd->kgtj/dot_general | solution.py:42
  93.0 8.4 %fusion.50 = f32[1,8,256,128]{3,2,1,0:T(8,128)S(1)} fusion(f32[512,256,8]{1,0,2:T(8,128)S(1)} %get-tuple-element.184, f32[8,256]{1,0:T(8,128)S(1)} %bitcast.153, pred[512]{0:T(512)(128)(4,1)S(1)} %add_compare_fusion.2, f32[1,8,256,128]{3,2,1,0:T(8,128)S(1)} %get-tuple-element.202, f32[8,256]{1,0:T(8,128)S(1)} %get-tuple-element.185, ...), kind=kOutput, calls=%fused_computation.12.clone.1 | convolution fusion | flops 1614282752 | bytes 6570500 | tf_op jit(solution)/shard_map/while/body/kgtj,jkd->kgtd/dot_general | solution.py:17
  101.4 0.9 fusion.49
  103.0 4.8 %bitcast_reduce_fusion.3 = (f32[8,256]{1,0:T(8,128)S(1)}, f32[512,256,8]{1,0,2:T(8,128)S(1)}) fusion(pred[512]{0:T(512)(128)(4,1)S(1)} %add_compare_fusion.2, f32[256,1,8,128]{3,0,2,1:T(8,128)S(1)} %get-tuple-element.219, f32[8,512,1,128]{3,1,2,0:T(8,128)} %get-tuple-element.218, s32[]{:T(128)S(6)} %select_n.45), kind=kOutput, calls=%fused_computation.3.clone.1 | convolution fusion | flops 1613756416 | bytes 5513732 | tf_op jit(solution)/shard_map/while/body/tkgd,jkd->kgtj/dot_general | solution.py:42
  107.8 8.4 %fusion.50 = f32[1,8,256,128]{3,2,1,0:T(8,128)S(1)} fusion(f32[512,256,8]{1,0,2:T(8,128)S(1)} %get-tuple-element.184, f32[8,256]{1,0:T(8,128)S(1)} %bitcast.153, pred[512]{0:T(512)(128)(4,1)S(1)} %add_compare_fusion.2, f32[1,8,256,128]{3,2,1,0:T(8,128)S(1)} %get-tuple-element.202, f32[8,256]{1,0:T(8,128)S(1)} %get-tuple-element.185, ...), kind=kOutput, calls=%fused_computation.12.clone.1 | convolution fusion | flops 1614282752 | bytes 6570500 | tf_op jit(solution)/shard_map/while/body/kgtj,jkd->kgtd/dot_general | solution.py:17
  116.2 0.9 fusion.49
  117.8 4.8 %bitcast_reduce_fusion.3 = (f32[8,256]{1,0:T(8,128)S(1)}, f32[512,256,8]{1,0,2:T(8,128)S(1)}) fusion(pred[512]{0:T(512)(128)(4,1)S(1)} %add_compare_fusion.2, f32[256,1,8,128]{3,0,2,1:T(8,128)S(1)} %get-tuple-element.219, f32[8,512,1,128]{3,1,2,0:T(8,128)} %get-tuple-element.218, s32[]{:T(128)S(6)} %select_n.45), kind=kOutput, calls=%fused_computation.3.clone.1 | convolution fusion | flops 1613756416 | bytes 5513732 | tf_op jit(solution)/shard_map/while/body/tkgd,jkd->kgtj/dot_general | solution.py:42
  122.6 8.4 %fusion.50 = f32[1,8,256,128]{3,2,1,0:T(8,128)S(1)} fusion(f32[512,256,8]{1,0,2:T(8,128)S(1)} %get-tuple-element.184, f32[8,256]{1,0:T(8,128)S(1)} %bitcast.153, pred[512]{0:T(512)(128)(4,1)S(1)} %add_compare_fusion.2, f32[1,8,256,128]{3,2,1,0:T(8,128)S(1)} %get-tuple-element.202, f32[8,256]{1,0:T(8,128)S(1)} %get-tuple-element.185, ...), kind=kOutput, calls=%fused_computation.12.clone.1 | convolution fusion | flops 1614282752 | bytes 6570500 | tf_op jit(solution)/shard_map/while/body/kgtj,jkd->kgtd/dot_general | solution.py:17
  131.0 0.9 fusion.49
  132.6 4.8 %bitcast_reduce_fusion.3 = (f32[8,256]{1,0:T(8,128)S(1)}, f32[512,256,8]{1,0,2:T(8,128)S(1)}) fusion(pred[512]{0:T(512)(128)(4,1)S(1)} %add_compare_fusion.2, f32[256,1,8,128]{3,0,2,1:T(8,128)S(1)} %get-tuple-element.219, f32[8,512,1,128]{3,1,2,0:T(8,128)} %get-tuple-element.218, s32[]{:T(128)S(6)} %select_n.45), kind=kOutput, calls=%fused_computation.3.clone.1 | convolution fusion | flops 1613756416 | bytes 5513732 | tf_op jit(solution)/shard_map/while/body/tkgd,jkd->kgtj/dot_general | solution.py:42
  137.4 8.4 %fusion.50 = f32[1,8,256,128]{3,2,1,0:T(8,128)S(1)} fusion(f32[512,256,8]{1,0,2:T(8,128)S(1)} %get-tuple-element.184, f32[8,256]{1,0:T(8,128)S(1)} %bitcast.153, pred[512]{0:T(512)(128)(4,1)S(1)} %add_compare_fusion.2, f32[1,8,256,128]{3,2,1,0:T(8,128)S(1)} %get-tuple-element.202, f32[8,256]{1,0:T(8,128)S(1)} %get-tuple-element.185, ...), kind=kOutput, calls=%fused_computation.12.clone.1 | convolution fusion | flops 1614282752 | bytes 6570500 | tf_op jit(solution)/shard_map/while/body/kgtj,jkd->kgtd/dot_general | solution.py:17
  145.8 0.9 fusion.49
  147.4 4.8 %bitcast_reduce_fusion.3 = (f32[8,256]{1,0:T(8,128)S(1)}, f32[512,256,8]{1,0,2:T(8,128)S(1)}) fusion(pred[512]{0:T(512)(128)(4,1)S(1)} %add_compare_fusion.2, f32[256,1,8,128]{3,0,2,1:T(8,128)S(1)} %get-tuple-element.219, f32[8,512,1,128]{3,1,2,0:T(8,128)} %get-tuple-element.218, s32[]{:T(128)S(6)} %select_n.45), kind=kOutput, calls=%fused_computation.3.clone.1 | convolution fusion | flops 1613756416 | bytes 5513732 | tf_op jit(solution)/shard_map/while/body/tkgd,jkd->kgtj/dot_general | solution.py:42
  152.2 8.4 %fusion.50 = f32[1,8,256,128]{3,2,1,0:T(8,128)S(1)} fusion(f32[512,256,8]{1,0,2:T(8,128)S(1)} %get-tuple-element.184, f32[8,256]{1,0:T(8,128)S(1)} %bitcast.153, pred[512]{0:T(512)(128)(4,1)S(1)} %add_compare_fusion.2, f32[1,8,256,128]{3,2,1,0:T(8,128)S(1)} %get-tuple-element.202, f32[8,256]{1,0:T(8,128)S(1)} %get-tuple-element.185, ...), kind=kOutput, calls=%fused_computation.12.clone.1 | convolution fusion | flops 1614282752 | bytes 6570500 | tf_op jit(solution)/shard_map/while/body/kgtj,jkd->kgtd/dot_general | solution.py:17
  160.6 0.9 fusion.49
  162.3 4.8 %bitcast_reduce_fusion.3 = (f32[8,256]{1,0:T(8,128)S(1)}, f32[512,256,8]{1,0,2:T(8,128)S(1)}) fusion(pred[512]{0:T(512)(128)(4,1)S(1)} %add_compare_fusion.2, f32[256,1,8,128]{3,0,2,1:T(8,128)S(1)} %get-tuple-element.219, f32[8,512,1,128]{3,1,2,0:T(8,128)} %get-tuple-element.218, s32[]{:T(128)S(6)} %select_n.45), kind=kOutput, calls=%fused_computation.3.clone.1 | convolution fusion | flops 1613756416 | bytes 5513732 | tf_op jit(solution)/shard_map/while/body/tkgd,jkd->kgtj/dot_general | solution.py:42
  167.0 8.4 %fusion.50 = f32[1,8,256,128]{3,2,1,0:T(8,128)S(1)} fusion(f32[512,256,8]{1,0,2:T(8,128)S(1)} %get-tuple-element.184, f32[8,256]{1,0:T(8,128)S(1)} %bitcast.153, pred[512]{0:T(512)(128)(4,1)S(1)} %add_compare_fusion.2, f32[1,8,256,128]{3,2,1,0:T(8,128)S(1)} %get-tuple-element.202, f32[8,256]{1,0:T(8,128)S(1)} %get-tuple-element.185, ...), kind=kOutput, calls=%fused_computation.12.clone.1 | convolution fusion | flops 1614282752 | bytes 6570500 | tf_op jit(solution)/shard_map/while/body/kgtj,jkd->kgtd/dot_general | solution.py:17
  177.1 4.8 %bitcast_reduce_fusion.3 = (f32[8,256]{1,0:T(8,128)S(1)}, f32[512,256,8]{1,0,2:T(8,128)S(1)}) fusion(pred[512]{0:T(512)(128)(4,1)S(1)} %add_compare_fusion.2, f32[256,1,8,128]{3,0,2,1:T(8,128)S(1)} %get-tuple-element.219, f32[8,512,1,128]{3,1,2,0:T(8,128)} %get-tuple-element.218, s32[]{:T(128)S(6)} %select_n.45), kind=kOutput, calls=%fused_computation.3.clone.1 | convolution fusion | flops 1613756416 | bytes 5513732 | tf_op jit(solution)/shard_map/while/body/tkgd,jkd->kgtj/dot_general | solution.py:42
  181.9 8.4 %fusion.50 = f32[1,8,256,128]{3,2,1,0:T(8,128)S(1)} fusion(f32[512,256,8]{1,0,2:T(8,128)S(1)} %get-tuple-element.184, f32[8,256]{1,0:T(8,128)S(1)} %bitcast.153, pred[512]{0:T(512)(128)(4,1)S(1)} %add_compare_fusion.2, f32[1,8,256,128]{3,2,1,0:T(8,128)S(1)} %get-tuple-element.202, f32[8,256]{1,0:T(8,128)S(1)} %get-tuple-element.185, ...), kind=kOutput, calls=%fused_computation.12.clone.1 | convolution fusion | flops 1614282752 | bytes 6570500 | tf_op jit(solution)/shard_map/while/body/kgtj,jkd->kgtd/dot_general | solution.py:17
  190.3 0.9 fusion.49
  192.2 20.5 %all-to-all-start.1 = ((f32[1,1,8,256]{2,1,0,3:T(1,128)}), f32[1,1,8,256]{2,1,0,3:T(1,128)S(1)}, u32[]{:S(2)}, u32[]{:S(2)}) async-start(f32[1,1,8,256]{2,1,0,3:T(1,128)} %bitcast.21), calls=%async_computation.1 | async-start | bytes 262144 | tf_op jit(solution)/shard_map/all_to_all | solution.py:57
  213.5 8.6 %all-to-all-done.1 = f32[1,1,8,256]{2,1,0,3:T(1,128)S(1)} async-done(((f32[1,1,8,256]{2,1,0,3:T(1,128)}), f32[1,1,8,256]{2,1,0,3:T(1,128)S(1)}, u32[]{:S(2)}, u32[]{:S(2)}) %all-to-all-start.1) | async-done | bytes 8224 | tf_op jit(solution)/shard_map/all_to_all | solution.py:57
  222.0 3.8 %all-to-all-start.2 = ((f32[1,1,8,256]{2,1,0,3:T(1,128)}), f32[1,1,8,256]{2,1,0,3:T(1,128)S(1)}, u32[]{:S(2)}, u32[]{:S(2)}) async-start(f32[1,1,8,256]{2,1,0,3:T(1,128)} %bitcast.31), calls=%async_computation.2 | async-start | bytes 262144 | tf_op jit(solution)/shard_map/all_to_all | solution.py:58
  225.9 1.6 copy.77
  227.5 7.8 %all-to-all-done.2 = f32[1,1,8,256]{2,1,0,3:T(1,128)S(1)} async-done(((f32[1,1,8,256]{2,1,0,3:T(1,128)}), f32[1,1,8,256]{2,1,0,3:T(1,128)S(1)}, u32[]{:S(2)}, u32[]{:S(2)}) %all-to-all-start.2) | async-done | bytes 8224 | tf_op jit(solution)/shard_map/all_to_all | solution.py:58
  235.3 3.9 %all-to-all-start = ((f32[1,1,8,256,128]{4,2,1,0,3:T(8,128)}), f32[1,1,8,256,128]{4,2,1,0,3:T(8,128)S(1)}, u32[]{:S(2)}, u32[]{:S(2)}) async-start(f32[1,1,8,256,128]{4,2,1,0,3:T(8,128)} %bitcast.123), calls=%async_computation | async-start | bytes 2097152 | tf_op jit(solution)/shard_map/all_to_all | solution.py:59
  239.3 45.1 %all_gather.10 = f32[256,128]{1,0:T(8,128)S(1)} all-gather(f32[8,128]{1,0:T(8,128)S(1)} %copy-done.1), channel_id=1, replica_groups=mesh['ctx'=32,'kvh'=8] {'ctx'}, dimensions={0}, use_global_device_ids=true | all-gather | bytes 135168 | tf_op jit(solution)/shard_map/all_gather | solution.py:66
  284.9 32.7 %all_gather.11 = f32[256,128]{1,0:T(8,128)S(1)} all-gather(f32[8,128]{1,0:T(8,128)S(1)} %copy-done.2), channel_id=1, replica_groups=mesh['ctx'=32,'kvh'=8] {'ctx'}, dimensions={0}, use_global_device_ids=true | all-gather | bytes 135168 | tf_op jit(solution)/shard_map/all_gather | solution.py:67
  319.1 34.0 %all_to_all.73 = f32[8,1,1024]{2,1,0:T(1,128)S(1)} all-to-all(f32[8,1,1024]{2,1,0:T(1,128)S(1)} %bitcast.162), channel_id=1, replica_groups=mesh['ctx'=32,'kvh'=8] {'kvh'}, dimensions={0} | all-to-all | bytes 65536 | tf_op jit(solution)/shard_map/all_to_all | solution.py:81
  (63 shorter events, 10.8 us)
Async XLA Ops:
  6.5 79.0 %all-gather.2.cloned.1.call-start = ((), (), s32[]{:S(2)}) async-start(), calls=%async_computation.4 | async-start | bytes 1081344 | tf_op jit(solution)/shard_map/all_gather | solution.py:30
  191.4 47.9 %copy-start.1 = (f32[8,128]{1,0:T(8,128)S(1)}, f32[8,128]{1,0:T(8,128)}, u32[]{:S(2)}) copy-start(f32[8,128]{1,0:T(8,128)} %param.11) | copy-start | bytes 12292
  191.4 93.0 %copy-start = (f32[8,1024]{1,0:T(8,128)S(1)}, f32[8,1024]{1,0:T(8,128)}, u32[]{:S(2)}) copy-start(f32[8,1024]{1,0:T(8,128)} %param.8) | copy-start | bytes 98308
  191.4 93.4 %copy-start.2 = (f32[8,128]{1,0:T(8,128)S(1)}, f32[8,128]{1,0:T(8,128)}, u32[]{:S(2)}) copy-start(f32[8,128]{1,0:T(8,128)} %param.12) | copy-start | bytes 12292
  192.2 29.8 %all-to-all-start.1 = ((f32[1,1,8,256]{2,1,0,3:T(1,128)}), f32[1,1,8,256]{2,1,0,3:T(1,128)S(1)}, u32[]{:S(2)}, u32[]{:S(2)}) async-start(f32[1,1,8,256]{2,1,0,3:T(1,128)} %bitcast.21), calls=%async_computation.1 | async-start | bytes 262144 | tf_op jit(solution)/shard_map/all_to_all | solution.py:57
  222.0 13.3 %all-to-all-start.2 = ((f32[1,1,8,256]{2,1,0,3:T(1,128)}), f32[1,1,8,256]{2,1,0,3:T(1,128)S(1)}, u32[]{:S(2)}, u32[]{:S(2)}) async-start(f32[1,1,8,256]{2,1,0,3:T(1,128)} %bitcast.31), calls=%async_computation.2 | async-start | bytes 262144 | tf_op jit(solution)/shard_map/all_to_all | solution.py:58
  235.3 83.2 %all-to-all-start = ((f32[1,1,8,256,128]{4,2,1,0,3:T(8,128)}), f32[1,1,8,256,128]{4,2,1,0,3:T(8,128)S(1)}, u32[]{:S(2)}, u32[]{:S(2)}) async-start(f32[1,1,8,256,128]{4,2,1,0,3:T(8,128)} %bitcast.123), calls=%async_computation | async-start | bytes 2097152 | tf_op jit(solution)/shard_map/all_to_all | solution.py:59
Sparse Core Ops, SparseCore 0:
  9.9 75.5 all-gather.1
where the time goes:
time: 362 us; the launch traced here: 361 us
  blocking collectives  112 us (31%)
  waiting for transfers between devices  94.7 us (26%)
  matrix products  92.6 us (26%)
  starting transfers between devices  28.3 us (8%)
  between operations  14.2 us (4%)
  other arithmetic  11.8 us (3%)
  local copies, waits for them, and re-layouts  6.42 us (2%)
    all_gather x1, waiting for transfers between devices, per_device(): whole_q = lax.all_gather(queries, 'ctx', axis=0, tiled=True)  77.6 us
    dot_general x8, matrix products, fold_block(): jnp.einsum('kgtj,jkd->kgtd', weights, values, precision=lax.Precision.HIG...  58.9 us
    all_gather x1, blocking collectives, per_device(): lax.all_gather(new_keys, 'ctx', axis=0, tiled=True)  45.1 us
    all_to_all x1, blocking collectives, per_device(): lax.all_to_all(result, 'kvh', split_axis=0, concat_axis=1, tiled=True)  34 us
    dot_general x7, matrix products, key_step(): jnp.einsum('tkgd,jkd->kgtj', query_heads, block_k, precision=lax.Precisio...  33.4 us
    all_gather x1, blocking collectives, per_device(): lax.all_gather(new_values, 'ctx', axis=0, tiled=True)  32.7 us
    all_to_all x1, starting transfers between devices, per_device(): lax.all_to_all(peak[None], 'ctx', split_axis=3, concat_axis=0, tiled=True)  20.5 us
    all_to_all x1, waiting for transfers between devices, per_device(): lax.all_to_all(peak[None], 'ctx', split_axis=3, concat_axis=0, tiled=True)  8.57 us
  transfers between devices with their start and end apart: 4, of which 3 were waited for; matrix products, arithmetic and copies ran while one was open for 1% of the time, Pallas kernels for 0%

commit v1 on v0

v1 whole, which is shorter than its diff:
```python
import functools
import math

import jax
import jax.numpy as jnp
from jax import lax
from jax.experimental import pallas as pl
from jax.experimental.pallas import tpu as pltpu
from jax.sharding import PartitionSpec as P

HQ = 64
KVH = 8
HD = 128
GROUP = HQ // KVH
NZ, NX = 8, 4
BLK = 4096
OWN = 8
ROWS = OWN * GROUP
R = NX * ROWS
PIECE = ROWS + 8
NEW = 128
T = 512
SCALE = math.log2(math.e) / math.sqrt(HD)
NEG = -1e30
MESH = pl.DeviceIdType.MESH
bf16, f32 = jnp.bfloat16, jnp.float32
NT = (((1,), (1,)), ((), ()))
NN = (((1,), (0,)), ((), ()))


def dot(a, b, dims):
    return lax.dot_general(a, b, dims, preferred_element_type=f32)


def split(x):
    high = x.astype(bf16)
    return high, (x - high.astype(f32)).astype(bf16)


def halves(k, first):
    return [(k, first), (k, first + 1), (-k, first), (-k, first + 1)]


CHUNKS = [
    [(0, i) for i in range(NX)],
    halves(1, 0),
    halves(2, 0),
    halves(3, 0),
    halves(3, 2),
    [(4, i) for i in range(NX)],
    halves(2, 2),
    halves(1, 2),
]
FORWARD = [(3, 1), (3, 2), (3, 3), (-3, 1), (-3, 2), (-3, 3), (4, 1), (4, 2), (4, 3)]
FAR = [1, -1, 2, -2, 3, -3, 4]
STRAIGHT = halves(1, 2) + halves(2, 2)
ALONG_X = {dz: [1] if abs(dz) < 3 else [1, 2, 3] for dz in FAR}
XSLOT = {pair: i for i, pair in enumerate([(0, k) for k in (1, 2, 3)] + [(dz, dx) for dz in FAR for dx in ALONG_X[dz]])}
DSLOT = {pair: i for i, pair in enumerate(STRAIGHT)}
ZSLOT = {dz: i for i, dz in enumerate(FAR)}


def kernel(
    q_ref, k_ref, v_ref, nk_ref, nv_ref, len_ref, o_ref,
    kbuf, vbuf, kc, vc, qbuf, nkv, sbuf, mbuf, own_o, own_l, own_m, part, xin, din, zout, zin, acc1, acc2,
    otmp, osend, oin,
    ksem, vsem, q_s, q_r, n_s, n_r, x_s, x_r, d_s, d_r, z_s, z_r, o_s, o_r,
):
    c = lax.axis_index("ctx")
    g = lax.axis_index("kvh")
    z, x = c // NX, c % NX

    def ctx_at(dz, dx):
        return {"ctx": ((z + dz + NZ) % NZ) * NX + (x + dx + NX) % NX}

    def remote(src, dst, ssem, rsem, dev):
        return pltpu.make_async_remote_copy(
            src_ref=src, dst_ref=dst, send_sem=ssem, recv_sem=rsem, device_id=dev, device_id_type=MESH
        )

    loads = []
    for i in range(4):
        rows = pl.ds(i * 1024, 1024)
        loads.append(
            (
                pltpu.make_async_copy(k_ref.at[rows], kbuf.at[rows], ksem.at[i]),
                pltpu.make_async_copy(v_ref.at[rows], vbuf.at[rows], vsem.at[i]),
            )
        )
    for one, two in loads:
        one.start()
        two.start()

    offsets = {(0, k) for k in (1, 2, 3)} | {(k, 0) for k in range(1, NZ)}
    for chunk in CHUNKS:
        for dz, dx in chunk:
            if (dz, dx) != (0, 0) and (dz, dx) not in FORWARD:
                offsets |= {(dz % NZ, dx % NX), (-dz % NZ, -dx % NX)}
    for dz, dx in STRAIGHT:
        offsets |= {(dz % NZ, dx % NX), (-dz % NZ, -dx % NX)}
    partners = [ctx_at(*pair) for pair in sorted(offsets, key=lambda pair: (min(pair[0], NZ - pair[0]), pair))]
    partners += [{"kvh": (g + k) % KVH} for k in range(1, KVH)]
    barrier = pltpu.get_barrier_semaphore()
    for dev in partners:
        pl.semaphore_signal(barrier, inc=1, device_id=dev, device_id_type=MESH)

    for h in range(GROUP):
        qbuf[z, x, h * OWN : (h + 1) * OWN, :] = q_ref[:, h * HD : (h + 1) * HD]
    nkv[z, 0:OWN, :] = nk_ref[...]
    nkv[z, OWN : 2 * OWN, :] = nv_ref[...]
    pl.semaphore_wait(barrier, len(partners))

    sent = []

    def go(copy):
        copy.start()
        sent.append(copy)

    def q_copy(dz, dx):
        return remote(
            qbuf.at[z, x], qbuf.at[z, x], q_s.at[dz % NZ, dx], q_r.at[dz % NZ, dx], ctx_at(-dz, -dx)
        )

    def q_pass(dz, dx):
        row = (z + dz + NZ) % NZ
        return remote(
            qbuf.at[row, x], qbuf.at[row, x], q_s.at[dz % NZ, dx], q_r.at[dz % NZ, dx], ctx_at(0, -dx)
        )

    def q_send(pairs):
        for dz, dx in pairs:
            if (dz, dx) != (0, 0) and (dz, dx) not in FORWARD:
                go(q_copy(dz, dx))

    waited = set()

    def q_wait(pairs):
        for pair in pairs:
            if pair != (0, 0) and pair not in waited:
                waited.add(pair)
                q_copy(*pair).wait_recv()

    def q_forward(dz):
        q_wait([(dz, 0)])
        for dx in (1, 2, 3):
            go(q_pass(dz, dx))

    filled = len_ref[0]

    def prep(i, _):
        r = pl.ds(pl.multiple_of(i * 256, 256), 256)
        high, low = split(kbuf[r, :])
        kc[r, 0:128] = high
        kc[r, 128:256] = high
        kc[r, 256:384] = low
        pos = i * 256 + lax.broadcasted_iota(jnp.int32, (256, 128), 0)
        lane = lax.broadcasted_iota(jnp.int32, (256, 128), 1)
        kc[r, 384:512] = jnp.where((lane == 0) & (pos >= filled), NEG, 0.0).astype(bf16)
        high, low = split(vbuf[r, :])
        vc[r, 0:128] = high
        vc[r, 128:256] = low
        return 0

    def prep_part(i):
        loads[i][0].wait()
        loads[i][1].wait()
        lax.fori_loop(i * 4, i * 4 + 4, prep, 0)

    def queries(p):
        rows = [qbuf[(z + dz + NZ) % NZ, (x + dx) % NX] for dz, dx in CHUNKS[p]]
        high, low = split(jnp.concatenate(rows, axis=0) * SCALE)
        lane = lax.broadcasted_iota(jnp.int32, (R, HD), 1)
        return jnp.concatenate([high, low, high, jnp.where(lane == 0, 1.0, 0.0).astype(bf16)], axis=1)

    def fold(s, m, vt, total, acc):
        width = s.shape[1]
        w = jnp.exp2(s - jnp.concatenate([m] * (width // 128), axis=1))
        for i in range(width // 128):
            total = total + w[:, i * 128 : (i + 1) * 128]
        high, low = split(w)
        return total, acc + dot(high, vt, NN) + dot(low, vt, NN)

    def finish(p, out, m, total):
        total = jnp.sum(total, axis=1, keepdims=True)
        lane = lax.broadcasted_iota(jnp.int32, (R, HD), 1)
        both = jnp.where(lane == 0, m, jnp.where(lane == 1, total, 0.0))
        for i in range(NX):
            part[p, i, 0:ROWS, :] = out[i * ROWS : (i + 1) * ROWS]
        for i in range(NX // 2):
            tile = both[i * 128 : (i + 1) * 128].T[0:8]
            part[p, 2 * i, ROWS:PIECE, :] = tile
            part[p, 2 * i + 1, ROWS:PIECE, :] = jnp.concatenate([tile[:, 64:], tile[:, :64]], axis=1)

    def phase(score, attend):
        if score is not None:
            qc = queries(score)
            mx = None
        if attend is not None:
            m = mbuf[attend % 2]
            total = jnp.zeros((R, HD), f32)
            acc = jnp.zeros((R, 2 * HD), f32)
        for j in range(BLK // T):
            t = slice(j * T, (j + 1) * T)
            if attend is not None:
                total, acc = fold(sbuf[:, t], m, vc[t, :], total, acc)
            if score is not None:
                s = dot(qc, kc[t, :], NT)
                sbuf[:, t] = s
                for i in range(T // 128):
                    one = s[:, i * 128 : (i + 1) * 128]
                    mx = one if mx is None else jnp.maximum(mx, one)
        if attend is not None:
            out = acc[:, :HD] + acc[:, HD:]
            if attend == 0:
                own_o[...] = out
                own_l[...] = total
                own_m[...] = m
            else:
                finish(attend, out, m, total)
        if score is not None:
            mbuf[score % 2] = jnp.broadcast_to(jnp.max(mx, axis=1, keepdims=True), (R, HD))

    def new_keys():
        kn = jnp.concatenate(
            [nkv[:, 0:OWN, :].reshape(NZ * OWN, HD), jnp.zeros((NEW - NZ * OWN, HD), f32)], axis=0
        )
        vn = jnp.concatenate(
            [nkv[:, OWN : 2 * OWN, :].reshape(NZ * OWN, HD), jnp.zeros((NEW - NZ * OWN, HD), f32)], axis=0
        )
        high, low = split(kn)
        s = dot(queries(0), jnp.concatenate([high, high, low, jnp.zeros((NEW, HD), bf16)], axis=1), NT)
        row = lax.broadcasted_iota(jnp.int32, (R, NEW), 0)
        col = lax.broadcasted_iota(jnp.int32, (R, NEW), 1)
        token = (z * NX + (x + row // ROWS) % NX) * OWN + row % OWN
        key = ((col // OWN) * NX + x) * OWN + col % OWN
        s = jnp.where((key <= token) & (col < NZ * OWN), s, NEG)
        old = own_m[...]
        m = jnp.maximum(old, jnp.max(s, axis=1, keepdims=True))
        factor = jnp.exp2(old - m)
        high, low = split(vn)
        total, acc = fold(
            s, m, jnp.concatenate([high, low], axis=1), own_l[...] * factor, jnp.zeros((R, 2 * HD), f32)
        )
        finish(0, own_o[...] * factor + acc[:, :HD] + acc[:, HD:], m, total)

    def x_copy(p, i):
        dz, dx = CHUNKS[p][i]
        n = XSLOT[dz, dx]
        return remote(part.at[p, i], xin.at[n], x_s.at[n], x_r.at[n], ctx_at(0, dx))

    def d_copy(p, i):
        dz, dx = CHUNKS[p][i]
        n = DSLOT[dz, dx]
        return remote(part.at[p, i], din.at[n], d_s.at[n], d_r.at[n], ctx_at(dz, dx))

    def z_copy(dz):
        n = ZSLOT[dz]
        return remote(zout.at[n], zin.at[n], z_s.at[n], z_r.at[n], ctx_at(dz, 0))

    arriving = {}

    def send(p):
        for i, pair in enumerate(CHUNKS[p]):
            if pair in XSLOT:
                arriving["x", pair] = x_copy(p, i)
                go(arriving["x", pair])
            if pair in DSLOT:
                arriving["d", pair] = d_copy(p, i)
                go(arriving["d", pair])

    def merge(pieces, last=False):
        tiles = [piece[ROWS:PIECE, :] for piece in pieces]
        peaks = [tile[0:1] for tile in tiles]
        top = functools.reduce(jnp.maximum, peaks)
        factors = [jnp.exp2(one - top) for one in peaks]
        total = functools.reduce(jnp.add, [f * tile[1:2] for f, tile in zip(factors, tiles)])
        if last:
            factors = [f / total for f in factors]
        pad = [jnp.zeros((1, HD), f32)] * (8 - len(factors))
        cols = jnp.concatenate(factors + pad, axis=0).T[0:ROWS]
        out = functools.reduce(
            jnp.add, [cols[:, i : i + 1] * piece[0:ROWS, :] for i, piece in enumerate(pieces)]
        )
        return out, jnp.concatenate([top, total, jnp.zeros((6, HD), f32)], axis=0)

    def merge_to(dst, pieces):
        out, tile = merge(pieces)
        dst[0:ROWS, :] = out
        dst[ROWS:PIECE, :] = tile

    where = {pair: (p, i) for p, chunk in enumerate(CHUNKS) for i, pair in enumerate(chunk)}

    def merge_x(dz):
        pieces = [part.at[where[dz, 0]]]
        for dx in ALONG_X[dz]:
            arriving["x", (dz, dx)].wait_recv()
            pieces.append(xin.at[XSLOT[dz, dx]])
        merge_to(zout.at[ZSLOT[dz]], pieces)
        arriving["z", dz] = z_copy(dz)
        go(arriving["z", dz])

    def z_wait(dz):
        arriving["z", dz].wait_recv()
        return zin.at[ZSLOT[dz]]

    def d_wait(pair):
        arriving["d", pair].wait_recv()
        return din.at[DSLOT[pair]]

    def x_wait(pair):
        arriving["x", pair].wait_recv()
        return xin.at[XSLOT[pair]]

    new_copies = [
        remote(nkv.at[z], nkv.at[z], n_s.at[k - 1], n_r.at[k - 1], ctx_at(k, 0)) for k in range(1, NZ)
    ]

    q_send(CHUNKS[0])
    q_send(CHUNKS[1])
    q_send([(3, 0), (-3, 0)])
    q_send(CHUNKS[2])
    for i in range(4):
        prep_part(i)
    q_send([(4, 0)])
    for copy in new_copies:
        go(copy)
    q_send(CHUNKS[6])
    q_send(CHUNKS[7])

    q_wait(CHUNKS[0])
    phase(0, None)
    phase(None, 0)
    q_wait(CHUNKS[1])
    phase(1, None)
    phase(None, 1)
    send(1)
    q_forward(3)
    q_forward(-3)
    q_wait(CHUNKS[2])
    phase(2, None)
    phase(None, 2)
    send(2)
    for copy in new_copies:
        copy.wait_recv()
    new_keys()
    send(0)
    q_forward(4)
    q_wait(CHUNKS[3])
    phase(3, None)
    merge_x(1)
    merge_x(-1)
    q_wait(CHUNKS[4])
    phase(4, 3)
    send(3)
    merge_x(2)
    merge_x(-2)
    q_wait(CHUNKS[5])
    phase(5, 4)
    send(4)
    q_wait(CHUNKS[6])
    phase(6, 5)
    send(5)
    merge_x(3)
    merge_x(-3)
    phase(None, 6)
    send(6)
    q_wait(CHUNKS[7])
    phase(7, None)
    phase(None, 7)
    send(7)
    merge_x(4)
    pieces = [part.at[0, 0]] + [x_wait((0, dx)) for dx in (1, 2, 3)] + [z_wait(dz) for dz in (1, -1, 2, -2)]
    merge_to(acc1, pieces)
    merge_to(acc2, [acc1] + [z_wait(dz) for dz in (3, -3)] + [d_wait(pair) for pair in halves(2, 2)])
    out, _ = merge([acc2] + [d_wait(pair) for pair in halves(1, 2)] + [z_wait(4)], last=True)

    otmp[...] = out
    for t in range(OWN):
        osend[t] = otmp[pl.ds(t, GROUP, stride=OWN), :]
    o_copies = []
    for k in range(1, KVH):
        there = (g + k) % KVH
        o_copies.append(remote(osend.at[there], oin.at[g], o_s.at[k - 1], o_r.at[k - 1], {"kvh": there}))
    for copy in o_copies:
        go(copy)
    oin[g] = osend[g]
    for copy in o_copies:
        copy.wait_recv()
    o_ref[...] = oin[...].reshape(HQ, HD)
    for copy in sent:
        copy.wait_send()


def per_device(queries, cache_keys, cache_values, new_keys, new_values, block_lengths):
    vmem = pl.BlockSpec(memory_space=pltpu.VMEM)
    hbm = pl.BlockSpec(memory_space=pl.ANY)
    dma = pltpu.SemaphoreType.DMA
    out = pl.pallas_call(
        kernel,
        out_shape=jax.ShapeDtypeStruct((HQ, HD), f32),
        in_specs=[vmem, hbm, hbm, vmem, vmem, pl.BlockSpec(memory_space=pltpu.SMEM)],
        out_specs=vmem,
        scratch_shapes=[
            pltpu.VMEM((BLK, HD), f32),
            pltpu.VMEM((BLK, HD), f32),
            pltpu.VMEM((BLK, 4 * HD), bf16),
            pltpu.VMEM((BLK, 2 * HD), bf16),
            pltpu.VMEM((NZ, NX, ROWS, HD), f32),
            pltpu.VMEM((NZ, 2 * OWN, HD), f32),
            pltpu.VMEM((R, BLK), f32),
            pltpu.VMEM((2, R, HD), f32),
            pltpu.VMEM((R, HD), f32),
            pltpu.VMEM((R, HD), f32),
            pltpu.VMEM((R, HD), f32),
            pltpu.VMEM((len(CHUNKS), NX, PIECE, HD), f32),
            pltpu.VMEM((len(XSLOT), PIECE, HD), f32),
            pltpu.VMEM((len(DSLOT), PIECE, HD), f32),
            pltpu.VMEM((len(ZSLOT), PIECE, HD), f32),
            pltpu.VMEM((len(ZSLOT), PIECE, HD), f32),
            pltpu.VMEM((PIECE, HD), f32),
            pltpu.VMEM((PIECE, HD), f32),
            pltpu.VMEM((ROWS, HD), f32),
            pltpu.VMEM((OWN, GROUP, HD), f32),
            pltpu.VMEM((KVH, GROUP, HD), f32),
            dma((4,)),
            dma((4,)),
            dma((NZ, NX)),
            dma((NZ, NX)),
            dma((NZ - 1,)),
            dma((NZ - 1,)),
            dma((len(XSLOT),)),
            dma((len(XSLOT),)),
            dma((len(DSLOT),)),
            dma((len(DSLOT),)),
            dma((len(ZSLOT),)),
            dma((len(ZSLOT),)),
            dma((KVH - 1,)),
            dma((KVH - 1,)),
        ],
        compiler_params=pltpu.CompilerParams(
            collective_id=0, has_side_effects=True, vmem_limit_bytes=56 * 1024 * 1024
        ),
        cost_estimate=pl.CostEstimate(
            flops=2 * 2 * 2048 * BLK * HD * 3, bytes_accessed=5 * 1024 * 1024, transcendentals=2048 * BLK
        ),
    )(queries, cache_keys, cache_values, new_keys, new_values, block_lengths)
    return out.reshape(1, HQ * HD)


def solution(mesh):
    in_specs = (P("ctx", "kvh"),) * 5 + (P("ctx"),)
    return jax.shard_map(
        per_device, mesh=mesh, in_specs=in_specs, out_specs=P(("ctx", "kvh"), None), check_vma=False
    )
```

time: 362 us -> 67.1 us (0.19)
  blocking collectives: 112 us -> 0 us
  waiting for transfers between devices: 94.7 us -> 0 us
  matrix products: 92.6 us -> 0 us
  Pallas kernels: 0 us -> 64.9 us
  starting transfers between devices: 28.3 us -> 0 us
  between operations: 14.2 us -> 0.66 us
  other arithmetic: 11.8 us -> 0 us
  local copies, waits for them, and re-layouts: 6.42 us -> 1.38 us
    dot_general x16 -> x0, matrix products: 92.6 us -> none  [the longest x8 58.9 us: fold_block(): jnp.einsum('kgtj,jkd->kgtd', weights, values, precision=lax.Precision.HIG...]
    all_gather x2 -> x0, blocking collectives: 77.8 us -> none  [the longest x1 45.1 us: per_device(): lax.all_gather(new_keys, 'ctx', axis=0, tiled=True)]
    all_gather x1 -> x0, waiting for transfers between devices: 77.6 us -> none  [per_device(): whole_q = lax.all_gather(queries, 'ctx', axis=0, tiled=True)]
    pallas_call x0 -> x1, Pallas kernels: none -> 64.9 us  [per_device(): pl.pallas_call(kernel, out_shape=jax.ShapeDtypeStruct((HQ, HD), f32), in_...]
    all_to_all x1 -> x0, blocking collectives: 34 us -> none  [per_device(): lax.all_to_all(result, 'kvh', split_axis=0, concat_axis=1, tiled=True)]
    all_to_all x3 -> x0, starting transfers between devices: 28.3 us -> none  [the longest x1 20.5 us: per_device(): lax.all_to_all(peak[None], 'ctx', split_axis=3, concat_axis=0, tiled=True)]
    all_to_all x3 -> x0, waiting for transfers between devices: 16.4 us -> none  [the longest x1 8.57 us: per_device(): lax.all_to_all(peak[None], 'ctx', split_axis=3, concat_axis=0, tiled=True)]
    reduce_sum x10 -> x0, other arithmetic: 6.92 us -> none  [the longest x8 6.54 us: fold_block(): total = total * factor + jnp.sum(weights, axis=-1)]
  transfers between devices with their start and end apart: 4 -> 0, of which waited for: 3 -> 0; matrix products, arithmetic and copies ran while one was open for 1% -> 0% of each run, Pallas kernels for 0% -> 0%
where the time goes in v1:
time: 67.1 us; the launch traced here: 66.9 us
  Pallas kernels  64.9 us (97%)
  local copies, waits for them, and re-layouts  1.38 us (2%)
    pallas_call x1, Pallas kernels, per_device(): pl.pallas_call(kernel, out_shape=jax.ShapeDtypeStruct((HQ, HD), f32), in_...  64.9 us
    unnamed x1, local copies, waits for them, and re-layouts  1.38 us

profile of v1, /device:TPU:1, one launch (start us, length us, event | category | flops | bytes accessed | tf_op | source)
XLA Modules:
  0.0 66.9 jit_solution(6779548503265084019)
XLA Ops:
  0.7 64.9 %shard_map.64 = f32[64,128]{1,0:T(8,128)} custom-call(f32[8,1024]{1,0:T(8,128)} %q_ref.1, f32[4096,128]{1,0:T(8,128)} %k_ref.1, f32[4096,128]{1,0:T(8,128)} %v_ref.1, f32[8,128]{1,0:T(8,128)} %nk_ref.1, f32[8,128]{1,0:T(8,128)} %nv_ref.1, s32[1]{0:T(128)S(6)} %copy.8.len_ref), custom_call_target="tpu_custom_call" | custom-call | flops 12884901888 | bytes 5242880 | tf_op jit(solution)/shard_map/pallas_call | solution.py:398
  65.5 1.4 %copy.9 = f32[1,8192]{1,0:T(1,128)} copy(f32[1,8192]{1,0:T(1,128)} %bitcast.1) | data formatting | bytes 65536

commit v2 on v1

--- a/solution.py
+++ b/solution.py
@@ -37,34 +37,18 @@
     return high, (x - high.astype(f32)).astype(bf16)
 
 
-def halves(k, first):
-    return [(k, first), (k, first + 1), (-k, first), (-k, first + 1)]
-
-
-CHUNKS = [
-    [(0, i) for i in range(NX)],
-    halves(1, 0),
-    halves(2, 0),
-    halves(3, 0),
-    halves(3, 2),
-    [(4, i) for i in range(NX)],
-    halves(2, 2),
-    halves(1, 2),
-]
-FORWARD = [(3, 1), (3, 2), (3, 3), (-3, 1), (-3, 2), (-3, 3), (4, 1), (4, 2), (4, 3)]
-FAR = [1, -1, 2, -2, 3, -3, 4]
-STRAIGHT = halves(1, 2) + halves(2, 2)
-ALONG_X = {dz: [1] if abs(dz) < 3 else [1, 2, 3] for dz in FAR}
-XSLOT = {pair: i for i, pair in enumerate([(0, k) for k in (1, 2, 3)] + [(dz, dx) for dz in FAR for dx in ALONG_X[dz]])}
-DSLOT = {pair: i for i, pair in enumerate(STRAIGHT)}
+ORDER = [0, 1, -1, 4, 3, -3, 2, -2]
+CHUNKS = [[(dz, i) for i in range(NX)] for dz in ORDER]
+FAR = ORDER[1:]
+XSLOT = {pair: i for i, pair in enumerate([(dz, dx) for dz in ORDER for dx in (1, 2, 3)])}
 ZSLOT = {dz: i for i, dz in enumerate(FAR)}
 
 
 def kernel(
     q_ref, k_ref, v_ref, nk_ref, nv_ref, len_ref, o_ref,
-    kbuf, vbuf, kc, vc, qbuf, nkv, sbuf, mbuf, own_o, own_l, own_m, part, xin, din, zout, zin, acc1, acc2,
+    kbuf, vbuf, kc, vc, qbuf, nkv, sbuf, mbuf, own_o, own_l, own_m, part, xin, zout, zin, acc1, acc2,
     otmp, osend, oin,
-    ksem, vsem, q_s, q_r, n_s, n_r, x_s, x_r, d_s, d_r, z_s, z_r, o_s, o_r,
+    ksem, vsem, q_s, q_r, n_s, n_r, x_s, x_r, z_s, z_r, o_s, o_r,
 ):
     c = lax.axis_index("ctx")
     g = lax.axis_index("kvh")
@@ -92,12 +76,6 @@
         two.start()
 
     offsets = {(0, k) for k in (1, 2, 3)} | {(k, 0) for k in range(1, NZ)}
-    for chunk in CHUNKS:
-        for dz, dx in chunk:
-            if (dz, dx) != (0, 0) and (dz, dx) not in FORWARD:
-                offsets |= {(dz % NZ, dx % NX), (-dz % NZ, -dx % NX)}
-    for dz, dx in STRAIGHT:
-        offsets |= {(dz % NZ, dx % NX), (-dz % NZ, -dx % NX)}
     partners = [ctx_at(*pair) for pair in sorted(offsets, key=lambda pair: (min(pair[0], NZ - pair[0]), pair))]
     partners += [{"kvh": (g + k) % KVH} for k in range(1, KVH)]
     barrier = pltpu.get_barrier_semaphore()
@@ -108,7 +86,6 @@
         qbuf[z, x, h * OWN : (h + 1) * OWN, :] = q_ref[:, h * HD : (h + 1) * HD]
     nkv[z, 0:OWN, :] = nk_ref[...]
     nkv[z, OWN : 2 * OWN, :] = nv_ref[...]
-    pl.semaphore_wait(barrier, len(partners))
 
     sent = []
 
@@ -116,34 +93,20 @@
         copy.start()
         sent.append(copy)
 
-    def q_copy(dz, dx):
-        return remote(
-            qbuf.at[z, x], qbuf.at[z, x], q_s.at[dz % NZ, dx], q_r.at[dz % NZ, dx], ctx_at(-dz, -dx)
-        )
-
-    def q_pass(dz, dx):
-        row = (z + dz + NZ) % NZ
-        return remote(
-            qbuf.at[row, x], qbuf.at[row, x], q_s.at[dz % NZ, dx], q_r.at[dz % NZ, dx], ctx_at(0, -dx)
-        )
-
-    def q_send(pairs):
-        for dz, dx in pairs:
-            if (dz, dx) != (0, 0) and (dz, dx) not in FORWARD:
-                go(q_copy(dz, dx))
-
-    waited = set()
-
-    def q_wait(pairs):
-        for pair in pairs:
-            if pair != (0, 0) and pair not in waited:
-                waited.add(pair)
-                q_copy(*pair).wait_recv()
-
-    def q_forward(dz):
-        q_wait([(dz, 0)])
-        for dx in (1, 2, 3):
-            go(q_pass(dz, dx))
+    def own_copy(dx):
+        return remote(qbuf.at[z, x], qbuf.at[z, x], q_s.at[0, dx], q_r.at[0, dx], ctx_at(0, -dx))
+
+    def row_copy(dz):
+        side = 1 if dz > 0 else -1
+        row = qbuf.at[(z + dz - side + NZ) % NZ]
+        return remote(row, row, q_s.at[dz % NZ, 0], q_r.at[dz % NZ, 0], ctx_at(-side, 0))
+
+    def far_copy(dz):
+        return remote(qbuf.at[z, x], qbuf.at[z, x], q_s.at[dz % NZ, 0], q_r.at[dz % NZ, 0], ctx_at(-dz, 0))
+
+    def pass_copy(dz, dx):
+        block = qbuf.at[(z + dz + NZ) % NZ, x]
+        return remote(block, block, q_s.at[dz % NZ, dx], q_r.at[dz % NZ, dx], ctx_at(0, -dx))
 
     filled = len_ref[0]
 
@@ -248,11 +211,6 @@
         n = XSLOT[dz, dx]
         return remote(part.at[p, i], xin.at[n], x_s.at[n], x_r.at[n], ctx_at(0, dx))
 
-    def d_copy(p, i):
-        dz, dx = CHUNKS[p][i]
-        n = DSLOT[dz, dx]
-        return remote(part.at[p, i], din.at[n], d_s.at[n], d_r.at[n], ctx_at(dz, dx))
-
     def z_copy(dz):
         n = ZSLOT[dz]
         return remote(zout.at[n], zin.at[n], z_s.at[n], z_r.at[n], ctx_at(dz, 0))
@@ -264,9 +222,6 @@
             if pair in XSLOT:
                 arriving["x", pair] = x_copy(p, i)
                 go(arriving["x", pair])
-            if pair in DSLOT:
-                arriving["d", pair] = d_copy(p, i)
-                go(arriving["d", pair])
 
     def merge(pieces, last=False):
         tiles = [piece[ROWS:PIECE, :] for piece in pieces]
@@ -292,21 +247,20 @@
 
     def merge_x(dz):
         pieces = [part.at[where[dz, 0]]]
-        for dx in ALONG_X[dz]:
+        for dx in (1, 2, 3):
             arriving["x", (dz, dx)].wait_recv()
             pieces.append(xin.at[XSLOT[dz, dx]])
         merge_to(zout.at[ZSLOT[dz]], pieces)
-        arriving["z", dz] = z_copy(dz)
-        go(arriving["z", dz])
+
+    def send_z(*dzs):
+        for dz in dzs:
+            arriving["z", dz] = z_copy(dz)
+            go(arriving["z", dz])
 
     def z_wait(dz):
         arriving["z", dz].wait_recv()
         return zin.at[ZSLOT[dz]]
 
-    def d_wait(pair):
-        arriving["d", pair].wait_recv()
-        return din.at[DSLOT[pair]]
-
     def x_wait(pair):
         arriving["x", pair].wait_recv()
         return xin.at[XSLOT[pair]]
@@ -315,64 +269,79 @@
         remote(nkv.at[z], nkv.at[z], n_s.at[k - 1], n_r.at[k - 1], ctx_at(k, 0)) for k in range(1, NZ)
     ]
 
-    q_send(CHUNKS[0])
-    q_send(CHUNKS[1])
-    q_send([(3, 0), (-3, 0)])
-    q_send(CHUNKS[2])
     for i in range(4):
         prep_part(i)
-    q_send([(4, 0)])
+    pl.semaphore_wait(barrier, len(partners))
+    own = [own_copy(dx) for dx in (1, 2, 3)]
+    for copy in own:
+        go(copy)
+    far = {dz: far_copy(dz) for dz in (4, 3, -3)}
+    for copy in far.values():
+        go(copy)
+    for copy in own:
+        copy.wait_recv()
+    rows = {dz: row_copy(dz) for dz in (1, -1, 2, -2)}
+    go(rows[1])
+    go(rows[-1])
+    phase(0, None)
+    phase(None, 0)
+    passed = {(dz, dx): pass_copy(dz, dx) for dz in far for dx in (1, 2, 3)}
+    for dz in far:
+        far[dz].wait_recv()
+        for dx in (1, 2, 3):
+            go(passed[dz, dx])
+    rows[1].wait_recv()
+    go(rows[2])
+    phase(1, None)
+    rows[-1].wait_recv()
+    go(rows[-2])
     for copy in new_copies:
         go(copy)
-    q_send(CHUNKS[6])
-    q_send(CHUNKS[7])
-
-    q_wait(CHUNKS[0])
-    phase(0, None)
-    phase(None, 0)
-    q_wait(CHUNKS[1])
-    phase(1, None)
-    phase(None, 1)
+    phase(2, 1)
     send(1)
-    q_forward(3)
-    q_forward(-3)
-    q_wait(CHUNKS[2])
-    phase(2, None)
-    phase(None, 2)
+
+    def wait_passed(dz):
+        for dx in (1, 2, 3):
+            passed[dz, dx].wait_recv()
+
+    wait_passed(4)
+    phase(3, 2)
     send(2)
+    wait_passed(3)
+    phase(4, 3)
+    send(3)
     for copy in new_copies:
         copy.wait_recv()
     new_keys()
     send(0)
-    q_forward(4)
-    q_wait(CHUNKS[3])
-    phase(3, None)
+    wait_passed(-3)
     merge_x(1)
-    merge_x(-1)
-    q_wait(CHUNKS[4])
-    phase(4, 3)
-    send(3)
-    merge_x(2)
-    merge_x(-2)
-    q_wait(CHUNKS[5])
     phase(5, 4)
     send(4)
-    q_wait(CHUNKS[6])
+    send_z(1)
+    rows[2].wait_recv()
+    merge_x(-1)
+    merge_x(4)
     phase(6, 5)
     send(5)
+    send_z(-1, 4)
+    rows[-2].wait_recv()
     merge_x(3)
-    merge_x(-3)
-    phase(None, 6)
+    phase(7, 6)
     send(6)
-    q_wait(CHUNKS[7])
-    phase(7, None)
+    send_z(3)
     phase(None, 7)
     send(7)
-    merge_x(4)
-    pieces = [part.at[0, 0]] + [x_wait((0, dx)) for dx in (1, 2, 3)] + [z_wait(dz) for dz in (1, -1, 2, -2)]
+    merge_x(-3)
+    send_z(-3)
+    pieces = [part.at[0, 0]] + [x_wait((0, dx)) for dx in (1, 2, 3)] + [z_wait(dz) for dz in (1, -1, 4)]
     merge_to(acc1, pieces)
-    merge_to(acc2, [acc1] + [z_wait(dz) for dz in (3, -3)] + [d_wait(pair) for pair in halves(2, 2)])
-    out, _ = merge([acc2] + [d_wait(pair) for pair in halves(1, 2)] + [z_wait(4)], last=True)
+    merge_x(2)
+    send_z(2)
+    merge_to(acc2, [acc1] + [z_wait(dz) for dz in (3, -3)])
+    merge_x(-2)
+    send_z(-2)
+    out, _ = merge([acc2, z_wait(2), z_wait(-2)], last=True)
 
     otmp[...] = out
     for t in range(OWN):
@@ -414,7 +383,6 @@
             pltpu.VMEM((R, HD), f32),
             pltpu.VMEM((len(CHUNKS), NX, PIECE, HD), f32),
             pltpu.VMEM((len(XSLOT), PIECE, HD), f32),
-            pltpu.VMEM((len(DSLOT), PIECE, HD), f32),
             pltpu.VMEM((len(ZSLOT), PIECE, HD), f32),
             pltpu.VMEM((len(ZSLOT), PIECE, HD), f32),
             pltpu.VMEM((PIECE, HD), f32),
@@ -430,8 +398,6 @@
             dma((NZ - 1,)),
             dma((len(XSLOT),)),
             dma((len(XSLOT),)),
-            dma((len(DSLOT),)),
-            dma((len(DSLOT),)),
             dma((len(ZSLOT),)),
             dma((len(ZSLOT),)),
             dma((KVH - 1,)),

time: 67.1 us -> 59.1 us (0.88)
  Pallas kernels: 64.9 us -> 56.8 us
    pallas_call x1, Pallas kernels: 64.9 us -> 56.8 us  [per_device(): pl.pallas_call(kernel, out_shape=jax.ShapeDtypeStruct((HQ, HD), f32), in_...]
where the time goes in v2:
time: 59.1 us; the launch traced here: 58.8 us
  Pallas kernels  56.8 us (96%)
  local copies, waits for them, and re-layouts  1.38 us (2%)
  between operations  0.66 us (1%)
    pallas_call x1, Pallas kernels, per_device(): pl.pallas_call(kernel, out_shape=jax.ShapeDtypeStruct((HQ, HD), f32), in_...  56.8 us
    unnamed x1, local copies, waits for them, and re-layouts  1.38 us

profile of v2, /device:TPU:1, one launch (start us, length us, event | category | flops | bytes accessed | tf_op | source)
XLA Modules:
  0.0 58.8 jit_solution(16219556622003854193)
XLA Ops:
  0.7 56.8 %shard_map.64 = f32[64,128]{1,0:T(8,128)} custom-call(f32[8,1024]{1,0:T(8,128)} %q_ref.1, f32[4096,128]{1,0:T(8,128)} %k_ref.1, f32[4096,128]{1,0:T(8,128)} %v_ref.1, f32[8,128]{1,0:T(8,128)} %nk_ref.1, f32[8,128]{1,0:T(8,128)} %nv_ref.1, s32[1]{0:T(128)S(6)} %copy.8.len_ref), custom_call_target="tpu_custom_call" | custom-call | flops 12884901888 | bytes 5242880 | tf_op jit(solution)/shard_map/pallas_call | solution.py:367
  57.5 1.4 %copy.9 = f32[1,8192]{1,0:T(1,128)} copy(f32[1,8192]{1,0:T(1,128)} %bitcast.1) | data formatting | bytes 65536

commit v3 on v2

--- a/solution.py
+++ b/solution.py
@@ -46,9 +46,9 @@
 
 def kernel(
     q_ref, k_ref, v_ref, nk_ref, nv_ref, len_ref, o_ref,
-    kbuf, vbuf, kc, vc, qbuf, nkv, sbuf, mbuf, own_o, own_l, own_m, part, xin, zout, zin, acc1, acc2,
-    otmp, osend, oin,
-    ksem, vsem, q_s, q_r, n_s, n_r, x_s, x_r, z_s, z_r, o_s, o_r,
+    qin, kbuf, vbuf, kc, vc, qbuf, nkv, sbuf, mbuf, own_o, own_l, own_m, part, xin, zout, zin, acc1,
+    otmp, omax, osend, oin,
+    in_s, ksem, vsem, q_s, q_r, n_s, n_r, x_s, x_r, z_s, z_r, o_s, o_r,
 ):
     c = lax.axis_index("ctx")
     g = lax.axis_index("kvh")
@@ -62,6 +62,21 @@
             src_ref=src, dst_ref=dst, send_sem=ssem, recv_sem=rsem, device_id=dev, device_id_type=MESH
         )
 
+    offsets = {(0, k) for k in (1, 2, 3)} | {(k, 0) for k in range(1, NZ)}
+    partners = [ctx_at(*pair) for pair in sorted(offsets, key=lambda pair: (min(pair[0], NZ - pair[0]), pair))]
+    partners += [{"kvh": (g + k) % KVH} for k in range(1, KVH)]
+    partners += [{**ctx_at(dz, 0), "kvh": (g + k) % KVH} for dz in (2, -2) for k in range(1, KVH)]
+    barrier = pltpu.get_barrier_semaphore()
+    for dev in partners:
+        pl.semaphore_signal(barrier, inc=1, device_id=dev, device_id_type=MESH)
+
+    firsts = [
+        pltpu.make_async_copy(q_ref, qin, in_s.at[0]),
+        pltpu.make_async_copy(nk_ref, nkv.at[z, 0:OWN], in_s.at[1]),
+        pltpu.make_async_copy(nv_ref, nkv.at[z, OWN : 2 * OWN], in_s.at[2]),
+    ]
+    for copy in firsts:
+        copy.start()
     loads = []
     for i in range(4):
         rows = pl.ds(i * 1024, 1024)
@@ -75,17 +90,10 @@
         one.start()
         two.start()
 
-    offsets = {(0, k) for k in (1, 2, 3)} | {(k, 0) for k in range(1, NZ)}
-    partners = [ctx_at(*pair) for pair in sorted(offsets, key=lambda pair: (min(pair[0], NZ - pair[0]), pair))]
-    partners += [{"kvh": (g + k) % KVH} for k in range(1, KVH)]
-    barrier = pltpu.get_barrier_semaphore()
-    for dev in partners:
-        pl.semaphore_signal(barrier, inc=1, device_id=dev, device_id_type=MESH)
-
+    for copy in firsts:
+        copy.wait()
     for h in range(GROUP):
-        qbuf[z, x, h * OWN : (h + 1) * OWN, :] = q_ref[:, h * HD : (h + 1) * HD]
-    nkv[z, 0:OWN, :] = nk_ref[...]
-    nkv[z, OWN : 2 * OWN, :] = nv_ref[...]
+        qbuf[z, x, h * OWN : (h + 1) * OWN, :] = qin[:, h * HD : (h + 1) * HD]
 
     sent = []
 
@@ -95,6 +103,10 @@
 
     def own_copy(dx):
         return remote(qbuf.at[z, x], qbuf.at[z, x], q_s.at[0, dx], q_r.at[0, dx], ctx_at(0, -dx))
+
+    def near_copy(dz, dx):
+        block = qbuf.at[z, (x + dx) % NX]
+        return remote(block, block, q_s.at[dz % NZ, dx], q_r.at[dz % NZ, dx], ctx_at(-dz, 0))
 
     def row_copy(dz):
         side = 1 if dz > 0 else -1
@@ -223,14 +235,12 @@
                 arriving["x", pair] = x_copy(p, i)
                 go(arriving["x", pair])
 
-    def merge(pieces, last=False):
+    def merge(pieces):
         tiles = [piece[ROWS:PIECE, :] for piece in pieces]
         peaks = [tile[0:1] for tile in tiles]
         top = functools.reduce(jnp.maximum, peaks)
         factors = [jnp.exp2(one - top) for one in peaks]
         total = functools.reduce(jnp.add, [f * tile[1:2] for f, tile in zip(factors, tiles)])
-        if last:
-            factors = [f / total for f in factors]
         pad = [jnp.zeros((1, HD), f32)] * (8 - len(factors))
         cols = jnp.concatenate(factors + pad, axis=0).T[0:ROWS]
         out = functools.reduce(
@@ -242,6 +252,34 @@
         out, tile = merge(pieces)
         dst[0:ROWS, :] = out
         dst[ROWS:PIECE, :] = tile
+
+    def merge_tokens(pieces, dst):
+        tiles = [piece[ROWS:PIECE, :] for piece in pieces]
+        peaks = [tile[0:1] for tile in tiles]
+        top = functools.reduce(jnp.maximum, peaks)
+        factors = [jnp.exp2(one - top) for one in peaks]
+        total = functools.reduce(jnp.add, [f * tile[1:2] for f, tile in zip(factors, tiles)])
+        n = len(factors)
+        pad = [jnp.zeros((1, HD), f32)] * (6 - n)
+        cols = jnp.concatenate(factors + [top, total] + pad, axis=0).T[0:ROWS]
+        otmp[...] = functools.reduce(
+            jnp.add, [cols[:, i : i + 1] * piece[0:ROWS, :] for i, piece in enumerate(pieces)]
+        )
+        lane = lax.broadcasted_iota(jnp.int32, (ROWS, HD), 1)
+        omax[...] = jnp.where(lane < HD // 2, cols[:, n : n + 1], cols[:, n + 1 : n + 2])
+        for t in range(OWN):
+            dst[t, 0:GROUP, :] = otmp[pl.ds(t, GROUP, stride=OWN), :]
+            dst[t, GROUP : 2 * GROUP, :] = omax[pl.ds(t, GROUP, stride=OWN), :]
+
+    def token_copies(n, dz):
+        copies = []
+        for k in range(0 if dz else 1, KVH):
+            there = (g + k) % KVH
+            dev = {**ctx_at(dz, 0), "kvh": there} if dz else {"kvh": there}
+            copies.append(remote(osend.at[n, there], oin.at[n, g], o_s.at[n, k], o_r.at[n, k], dev))
+        for copy in copies:
+            copy.start()
+        return copies
 
     where = {pair: (p, i) for p, chunk in enumerate(CHUNKS) for i, pair in enumerate(chunk)}
 
@@ -278,11 +316,14 @@
     far = {dz: far_copy(dz) for dz in (4, 3, -3)}
     for copy in far.values():
         go(copy)
-    for copy in own:
-        copy.wait_recv()
-    rows = {dz: row_copy(dz) for dz in (1, -1, 2, -2)}
-    go(rows[1])
-    go(rows[-1])
+    near = {(dz, dx): near_copy(dz, dx) for dz in (1, -1) for dx in range(NX)}
+    go(near[1, 0])
+    go(near[-1, 0])
+    for dx in (1, 3, 2):
+        own[dx - 1].wait_recv()
+        go(near[1, dx])
+        go(near[-1, dx])
+    rows = {dz: row_copy(dz) for dz in (2, -2)}
     phase(0, None)
     phase(None, 0)
     passed = {(dz, dx): pass_copy(dz, dx) for dz in far for dx in (1, 2, 3)}
@@ -290,10 +331,12 @@
         far[dz].wait_recv()
         for dx in (1, 2, 3):
             go(passed[dz, dx])
-    rows[1].wait_recv()
+    for dx in range(NX):
+        near[1, dx].wait_recv()
     go(rows[2])
     phase(1, None)
-    rows[-1].wait_recv()
+    for dx in range(NX):
+        near[-1, dx].wait_recv()
     go(rows[-2])
     for copy in new_copies:
         go(copy)
@@ -336,27 +379,28 @@
     send_z(-3)
     pieces = [part.at[0, 0]] + [x_wait((0, dx)) for dx in (1, 2, 3)] + [z_wait(dz) for dz in (1, -1, 4)]
     merge_to(acc1, pieces)
-    merge_x(2)
-    send_z(2)
-    merge_to(acc2, [acc1] + [z_wait(dz) for dz in (3, -3)])
-    merge_x(-2)
-    send_z(-2)
-    out, _ = merge([acc2, z_wait(2), z_wait(-2)], last=True)
-
-    otmp[...] = out
-    for t in range(OWN):
-        osend[t] = otmp[pl.ds(t, GROUP, stride=OWN), :]
-    o_copies = []
-    for k in range(1, KVH):
-        there = (g + k) % KVH
-        o_copies.append(remote(osend.at[there], oin.at[g], o_s.at[k - 1], o_r.at[k - 1], {"kvh": there}))
-    for copy in o_copies:
-        go(copy)
-    oin[g] = osend[g]
+    def pieces_x(dz):
+        return [part.at[where[dz, 0]]] + [x_wait((dz, dx)) for dx in (1, 2, 3)]
+
+    merge_tokens(pieces_x(2), osend.at[1])
+    o_copies = token_copies(1, 2)
+    merge_tokens(pieces_x(-2), osend.at[2])
+    o_copies += token_copies(2, -2)
+    merge_tokens([acc1] + [z_wait(dz) for dz in (3, -3)], osend.at[0])
+    o_copies += token_copies(0, 0)
+    oin[0, g] = osend[0, g]
+    for copy in sent:
+        copy.wait_send()
     for copy in o_copies:
         copy.wait_recv()
-    o_ref[...] = oin[...].reshape(HQ, HD)
-    for copy in sent:
+    outs = [oin[n, :, 0:GROUP, :].reshape(HQ, HD) for n in range(3)]
+    tiles = [oin[n, :, GROUP : 2 * GROUP, :].reshape(HQ, HD) for n in range(3)]
+    peaks = [tile[:, 0:1] for tile in tiles]
+    top = functools.reduce(jnp.maximum, peaks)
+    factors = [jnp.exp2(one - top) for one in peaks]
+    total = functools.reduce(jnp.add, [f * tile[:, HD // 2 : HD // 2 + 1] for f, tile in zip(factors, tiles)])
+    o_ref[...] = functools.reduce(jnp.add, [f * out for f, out in zip(factors, outs)]) / total
+    for copy in o_copies:
         copy.wait_send()
 
 
@@ -367,9 +411,10 @@
     out = pl.pallas_call(
         kernel,
         out_shape=jax.ShapeDtypeStruct((HQ, HD), f32),
-        in_specs=[vmem, hbm, hbm, vmem, vmem, pl.BlockSpec(memory_space=pltpu.SMEM)],
+        in_specs=[hbm, hbm, hbm, hbm, hbm, pl.BlockSpec(memory_space=pltpu.SMEM)],
         out_specs=vmem,
         scratch_shapes=[
+            pltpu.VMEM((OWN, GROUP * HD), f32),
             pltpu.VMEM((BLK, HD), f32),
             pltpu.VMEM((BLK, HD), f32),
             pltpu.VMEM((BLK, 4 * HD), bf16),
@@ -386,10 +431,11 @@
             pltpu.VMEM((len(ZSLOT), PIECE, HD), f32),
             pltpu.VMEM((len(ZSLOT), PIECE, HD), f32),
             pltpu.VMEM((PIECE, HD), f32),
-            pltpu.VMEM((PIECE, HD), f32),
             pltpu.VMEM((ROWS, HD), f32),
-            pltpu.VMEM((OWN, GROUP, HD), f32),
-            pltpu.VMEM((KVH, GROUP, HD), f32),
+            pltpu.VMEM((ROWS, HD), f32),
+            pltpu.VMEM((3, OWN, 2 * GROUP, HD), f32),
+            pltpu.VMEM((3, KVH, 2 * GROUP, HD), f32),
+            dma((3,)),
             dma((4,)),
             dma((4,)),
             dma((NZ, NX)),
@@ -400,8 +446,8 @@
             dma((len(XSLOT),)),
             dma((len(ZSLOT),)),
             dma((len(ZSLOT),)),
-            dma((KVH - 1,)),
-            dma((KVH - 1,)),
+            dma((3, KVH)),
+            dma((3, KVH)),
         ],
         compiler_params=pltpu.CompilerParams(
             collective_id=0, has_side_effects=True, vmem_limit_bytes=56 * 1024 * 1024

time: 59.1 us -> 56.6 us (0.958)
  Pallas kernels: 56.8 us -> 54.4 us
    pallas_call x1, Pallas kernels: 56.8 us -> 54.4 us  [per_device(): pl.pallas_call(kernel, out_shape=jax.ShapeDtypeStruct((HQ, HD), f32), in_...]
where the time goes in v3:
time: 56.6 us; the launch traced here: 56.4 us
  Pallas kernels  54.4 us (96%)
  local copies, waits for them, and re-layouts  1.38 us (2%)
  between operations  0.66 us (1%)
    pallas_call x1, Pallas kernels, per_device(): pl.pallas_call(kernel, out_shape=jax.ShapeDtypeStruct((HQ, HD), f32), in_...  54.4 us
    unnamed x1, local copies, waits for them, and re-layouts  1.38 us

profile of v3, /device:TPU:1, one launch (start us, length us, event | category | flops | bytes accessed | tf_op | source)
XLA Modules:
  0.0 56.4 jit_solution(16080770198863338916)
XLA Ops:
  0.7 54.4 %shard_map.64 = f32[64,128]{1,0:T(8,128)} custom-call(f32[8,1024]{1,0:T(8,128)} %q_ref.1, f32[4096,128]{1,0:T(8,128)} %k_ref.1, f32[4096,128]{1,0:T(8,128)} %v_ref.1, f32[8,128]{1,0:T(8,128)} %nk_ref.1, f32[8,128]{1,0:T(8,128)} %nv_ref.1, s32[1]{0:T(128)S(6)} %copy.8.len_ref), custom_call_target="tpu_custom_call" | custom-call | flops 12884901888 | bytes 5242880 | tf_op jit(solution)/shard_map/pallas_call | solution.py:411
  55.0 1.4 %copy.9 = f32[1,8192]{1,0:T(1,128)} copy(f32[1,8192]{1,0:T(1,128)} %bitcast.1) | data formatting | bytes 65536

commit v4 on v3

--- a/solution.py
+++ b/solution.py
@@ -283,10 +283,14 @@
 
     where = {pair: (p, i) for p, chunk in enumerate(CHUNKS) for i, pair in enumerate(chunk)}
 
+    def wait_x(*dzs):
+        for dz in dzs:
+            for dx in (1, 2, 3):
+                arriving["x", (dz, dx)].wait_recv()
+
     def merge_x(dz):
         pieces = [part.at[where[dz, 0]]]
         for dx in (1, 2, 3):
-            arriving["x", (dz, dx)].wait_recv()
             pieces.append(xin.at[XSLOT[dz, dx]])
         merge_to(zout.at[ZSLOT[dz]], pieces)
 
@@ -355,26 +359,30 @@
     send(3)
     for copy in new_copies:
         copy.wait_recv()
+    wait_passed(-3)
+    wait_x(1)
     new_keys()
-    send(0)
-    wait_passed(-3)
     merge_x(1)
     phase(5, 4)
     send(4)
+    send(0)
     send_z(1)
     rows[2].wait_recv()
+    wait_x(-1, 4)
     merge_x(-1)
     merge_x(4)
     phase(6, 5)
     send(5)
     send_z(-1, 4)
     rows[-2].wait_recv()
+    wait_x(3)
     merge_x(3)
     phase(7, 6)
     send(6)
     send_z(3)
     phase(None, 7)
     send(7)
+    wait_x(-3)
     merge_x(-3)
     send_z(-3)
     pieces = [part.at[0, 0]] + [x_wait((0, dx)) for dx in (1, 2, 3)] + [z_wait(dz) for dz in (1, -1, 4)]

time: 56.6 us -> 56.7 us (level)
  no operation moved by 1% of the time
where the time goes in v4:
time: 56.7 us; the launch traced here: 56.5 us
  Pallas kernels  54.5 us (96%)
  local copies, waits for them, and re-layouts  1.38 us (2%)
  between operations  0.66 us (1%)
    pallas_call x1, Pallas kernels, per_device(): pl.pallas_call(kernel, out_shape=jax.ShapeDtypeStruct((HQ, HD), f32), in_...  54.5 us
    unnamed x1, local copies, waits for them, and re-layouts  1.38 us

profile of v4, /device:TPU:1, one launch (start us, length us, event | category | flops | bytes accessed | tf_op | source)
XLA Modules:
  0.0 56.5 jit_solution(17306478134510435959)
XLA Ops:
  0.7 54.5 %shard_map.64 = f32[64,128]{1,0:T(8,128)} custom-call(f32[8,1024]{1,0:T(8,128)} %q_ref.1, f32[4096,128]{1,0:T(8,128)} %k_ref.1, f32[4096,128]{1,0:T(8,128)} %v_ref.1, f32[8,128]{1,0:T(8,128)} %nk_ref.1, f32[8,128]{1,0:T(8,128)} %nv_ref.1, s32[1]{0:T(128)S(6)} %copy.8.len_ref), custom_call_target="tpu_custom_call" | custom-call | flops 12884901888 | bytes 5242880 | tf_op jit(solution)/shard_map/pallas_call | solution.py:419
  55.1 1.4 %copy.9 = f32[1,8192]{1,0:T(1,128)} copy(f32[1,8192]{1,0:T(1,128)} %bitcast.1) | data formatting | bytes 65536

commit v5 on v3

--- a/solution.py
+++ b/solution.py
@@ -362,22 +362,25 @@
     phase(5, 4)
     send(4)
     send_z(1)
+    merge_x(-1)
+    phase(None, 5)
+    send(5)
+    send_z(-1)
     rows[2].wait_recv()
-    merge_x(-1)
+    phase(6, None)
     merge_x(4)
-    phase(6, 5)
-    send(5)
-    send_z(-1, 4)
+    phase(None, 6)
+    send(6)
+    send_z(4)
     rows[-2].wait_recv()
+    phase(7, None)
     merge_x(3)
-    phase(7, 6)
-    send(6)
     send_z(3)
     phase(None, 7)
     send(7)
     merge_x(-3)
     send_z(-3)
-    pieces = [part.at[0, 0]] + [x_wait((0, dx)) for dx in (1, 2, 3)] + [z_wait(dz) for dz in (1, -1, 4)]
+    pieces = [part.at[0, 0]] + [x_wait((0, dx)) for dx in (1, 2, 3)] + [z_wait(dz) for dz in (1, -1)]
     merge_to(acc1, pieces)
     def pieces_x(dz):
         return [part.at[where[dz, 0]]] + [x_wait((dz, dx)) for dx in (1, 2, 3)]
@@ -386,7 +389,7 @@
     o_copies = token_copies(1, 2)
     merge_tokens(pieces_x(-2), osend.at[2])
     o_copies += token_copies(2, -2)
-    merge_tokens([acc1] + [z_wait(dz) for dz in (3, -3)], osend.at[0])
+    merge_tokens([acc1] + [z_wait(dz) for dz in (4, 3, -3)], osend.at[0])
     o_copies += token_copies(0, 0)
     oin[0, g] = osend[0, g]
     for copy in sent:

time: 56.6 us -> 59.5 us (1.051)
  Pallas kernels: 54.4 us -> 57.3 us
    pallas_call x1, Pallas kernels: 54.4 us -> 57.3 us  [per_device(): pl.pallas_call(kernel, out_shape=jax.ShapeDtypeStruct((HQ, HD), f32), in_...]
where the time goes in v5:
time: 59.5 us; the launch traced here: 59.3 us
  Pallas kernels  57.3 us (96%)
  local copies, waits for them, and re-layouts  1.38 us (2%)
  between operations  0.66 us (1%)
    pallas_call x1, Pallas kernels, per_device(): pl.pallas_call(kernel, out_shape=jax.ShapeDtypeStruct((HQ, HD), f32), in_...  57.3 us
    unnamed x1, local copies, waits for them, and re-layouts  1.38 us

profile of v5, /device:TPU:1, one launch (start us, length us, event | category | flops | bytes accessed | tf_op | source)
XLA Modules:
  0.0 59.3 jit_solution(10020435088086978815)
XLA Ops:
  0.7 57.3 %shard_map.64 = f32[64,128]{1,0:T(8,128)} custom-call(f32[8,1024]{1,0:T(8,128)} %q_ref.1, f32[4096,128]{1,0:T(8,128)} %k_ref.1, f32[4096,128]{1,0:T(8,128)} %v_ref.1, f32[8,128]{1,0:T(8,128)} %nk_ref.1, f32[8,128]{1,0:T(8,128)} %nv_ref.1, s32[1]{0:T(128)S(6)} %copy.8.len_ref), custom_call_target="tpu_custom_call" | custom-call | flops 12884901888 | bytes 5242880 | tf_op jit(solution)/shard_map/pallas_call | solution.py:414
  58.0 1.4 %copy.9 = f32[1,8192]{1,0:T(1,128)} copy(f32[1,8192]{1,0:T(1,128)} %bitcast.1) | data formatting | bytes 65536
